TPU v7x, 32 devices: a whole 2x2x4 slice. The times are simulated.
32 devices in a mesh: dp: 2 (over y), expert: 16 (over z, x, core).
Axes of the slice: x: 2, y: 2, z: 4, core: 2. Of those that a mesh axis runs over, the one named last changes fastest.
Arguments:
- tokens: bfloat16 [6144, 2048], P(('dp', 'expert')), may hold values from -6 to 6
- routing: int32 [6144, 1], P(('dp', 'expert')), may hold values from 0 to 15; in each aligned block of 192 rows (0 to 191, 192 to 383, ...) at most 24 rows name the same one
- gate_scale: float32 [6144, 1], P(('dp', 'expert')), may hold values from 0.25 to 1
- cotangent: bfloat16 [6144, 2048], P(('dp', 'expert')), may hold values from -6 to 6
- up_weight: bfloat16 [16, 512, 2048], P('expert', 'dp'), may hold values from -0.125 to 0.125
- down_weight: bfloat16 [16, 512, 2048], P('expert', 'dp'), may hold values from -0.25 to 0.25
Outputs:
- output_rows: bfloat16 [6144, 2048], P(('dp', 'expert'))
- token_grad: bfloat16 [6144, 2048], P(('dp', 'expert'))
- grad_up: bfloat16 [16, 512, 2048], P('expert', 'dp')
- grad_down: bfloat16 [16, 512, 2048], P('expert', 'dp')
Inputs may be any that keep to these rules, and one draw needn't show every extreme that they name: `routing`: within the 192 tokens of one device, each expert is named by at most 24 tokens, a bound that some block reaches.
All inputs are finite; a program needn't handle non-finite values.
Results may differ from a plain program's by a relative error of at most 0.014.
Values may be sent and summed in bfloat16 or wider, within the bound.
A program may use at most 64 MiB of HBM per device.

v0:
```python
import jax
import jax.numpy as jnp
from jax import lax
from jax.sharding import PartitionSpec as P


def smooth(values):
    return jax.nn.gelu(values, approximate=True)


def contract_rows(left, right):
    return lax.dot_general(
        left, right, (((0,), (0,)), ((), ())), preferred_element_type=jnp.float32
    )


def contract_cols(left, right):
    return lax.dot_general(
        left, right, (((1,), (1,)), ((), ())), preferred_element_type=jnp.float32
    )


def per_device(tokens, routing, gate_scale, cotangent, up_weight, down_weight):
    tok_count = tokens.shape[0]
    width = tokens.shape[1]
    n_expert = lax.axis_size("expert")
    capacity = 2 * tok_count // n_expert
    slot_total = n_expert * capacity
    ids = routing[:, 0]
    onehot = (ids[:, None] == jnp.arange(n_expert, dtype=jnp.int32)[None, :]).astype(jnp.float32)
    position = jnp.arange(tok_count, dtype=jnp.int32)
    lower_tri = (position[:, None] >= position[None, :]).astype(jnp.float32)
    counts = jnp.dot(
        lower_tri, onehot, precision=lax.Precision.HIGHEST, preferred_element_type=jnp.float32
    )
    slot_rank = (jnp.sum(counts * onehot, axis=1) - 1.0).astype(jnp.int32)
    slot_index = ids * capacity + slot_rank
    placer = (jnp.arange(slot_total, dtype=jnp.int32)[:, None] == slot_index[None, :]).astype(
        jnp.bfloat16
    )

    def place(values):
        placed = jnp.dot(placer, values, preferred_element_type=jnp.float32).astype(jnp.bfloat16)
        return placed.reshape(n_expert, capacity, width)

    scaled = (gate_scale * cotangent.astype(jnp.float32)).astype(jnp.bfloat16)
    arrived_tok = lax.all_to_all(place(tokens), "expert", split_axis=0, concat_axis=0, tiled=True)
    slot_rows = arrived_tok.reshape(slot_total, width)
    up_all, down_all = (
        lax.all_gather(up_weight, "dp", axis=1, tiled=True),
        lax.all_gather(down_weight, "dp", axis=1, tiled=True),
    )
    preact = contract_cols(slot_rows, up_all[0])
    hidden = smooth(preact).astype(jnp.bfloat16)
    expert_out = jnp.dot(hidden, down_all[0], preferred_element_type=jnp.float32).astype(
        jnp.bfloat16
    )
    returned = lax.all_to_all(
        expert_out.reshape(n_expert, capacity, width),
        "expert",
        split_axis=0,
        concat_axis=0,
        tiled=True,
    )
    picked = contract_rows(placer, returned.reshape(slot_total, width))
    output_rows = (gate_scale * picked).astype(jnp.bfloat16)
    arrived_cot = lax.all_to_all(place(scaled), "expert", split_axis=0, concat_axis=0, tiled=True)
    cot_rows = arrived_cot.reshape(slot_total, width)
    hidden_grad = contract_cols(cot_rows, down_all[0])
    unused, backward = jax.vjp(smooth, preact)
    preact_grad = backward(hidden_grad)[0].astype(jnp.bfloat16)
    slot_grad = jnp.dot(preact_grad, up_all[0], preferred_element_type=jnp.float32).astype(
        jnp.bfloat16
    )
    grad_back = lax.all_to_all(
        slot_grad.reshape(n_expert, capacity, width),
        "expert",
        split_axis=0,
        concat_axis=0,
        tiled=True,
    )
    token_grad = contract_rows(placer, grad_back.reshape(slot_total, width)).astype(jnp.bfloat16)
    term_up = contract_rows(preact_grad, slot_rows)
    term_down = contract_rows(hidden, cot_rows)
    summed_terms = lax.psum_scatter(
        jnp.stack((term_up, term_down), axis=1).astype(jnp.bfloat16),
        "dp",
        scatter_dimension=0,
        tiled=True,
    ).astype(jnp.float32)
    grad_up = summed_terms[:, 0, :].astype(jnp.bfloat16)[None]
    grad_down = summed_terms[:, 1, :].astype(jnp.bfloat16)[None]
    return (output_rows, token_grad, grad_up, grad_down)


def solution(mesh):
    return jax.shard_map(
        per_device,
        mesh=mesh,
        in_specs=(
            P(("dp", "expert"), None),
            P(("dp", "expert"), None),
            P(("dp", "expert"), None),
            P(("dp", "expert"), None),
            P("expert", "dp", None),
            P("expert", "dp", None),
        ),
        out_specs=(
            P(("dp", "expert"), None),
            P(("dp", "expert"), None),
            P("expert", "dp", None),
            P("expert", "dp", None),
        ),
        check_vma=False,
    )
```

profile of v0, /device:TPU:11, one launch (start us, length us, event | category | flops | bytes accessed | tf_op | source)
XLA Modules:
  0.0 203.7 jit_solution(7905995586372793309)
XLA Ops:
  7.2 0.0 copy-start
  7.2 0.9 fusion.9
  8.1 0.7 convert_add_fusion
  8.8 1.7 convolution_convert_fusion.5
  10.6 6.7 %all-to-all-start = ((bf16[16,24,2048]{2,1,0:T(8,128)(2,1)}), bf16[16,24,2048]{2,1,0:T(8,128)(2,1)S(1)}, u32[]{:S(2)}, u32[]{:S(2)}) async-start(bf16[16,24,2048]{2,1,0:T(8,128)(2,1)} %bitcast.2), calls=%async_computation | async-start | bytes 3145728 | tf_op jit(solution)/shard_map/all_to_all | solution.py:47
  17.3 0.0 all-gather.3.cloned.1.call-start
  17.3 0.7 all-gather.3.cloned.1.call-update
  18.0 1.8 convolution_convert_fusion.3
  19.8 33.8 %all-to-all-done = bf16[16,24,2048]{2,1,0:T(8,128)(2,1)S(1)} async-done(((bf16[16,24,2048]{2,1,0:T(8,128)(2,1)}), bf16[16,24,2048]{2,1,0:T(8,128)(2,1)S(1)}, u32[]{:S(2)}, u32[]{:S(2)}) %all-to-all-start) | async-done | bytes 1572896 | tf_op jit(solution)/shard_map/all_to_all | solution.py:47
  53.6 4.8 %all-to-all-start.2 = ((bf16[16,24,2048]{2,1,0:T(8,128)(2,1)}), bf16[16,24,2048]{2,1,0:T(8,128)(2,1)}, u32[]{:S(2)}, u32[]{:S(2)}) async-start(bf16[16,24,2048]{2,1,0:T(8,128)(2,1)} %bitcast.8), calls=%async_computation.2 | async-start | bytes 3145728 | tf_op jit(solution)/shard_map/all_to_all | solution.py:67
  58.4 0.0 all-gather.5.cloned.1.call-start
  58.4 0.7 all-gather.5.cloned.1.call-update
  59.1 0.0 reduce-scatter.2.cloned.1.call-start
  59.1 0.0 all-gather.3.cloned.1.call-done
  59.2 3.5 %fusion.7 = f32[384,512]{1,0:T(8,128)} fusion(bf16[384,2048]{1,0:T(8,128)(2,1)S(1)} %bitcast.40, bf16[1,512,2048]{2,1,0:T(8,128)(2,1)} %all-gather.3.cloned.1.call-done), kind=kOutput, calls=%fused_computation.16 | convolution fusion | flops 805306368 | bytes 4456448 | tf_op jit(solution)/shard_map/dot_general | solution.py:18
  62.7 32.0 %all-to-all-done.2 = bf16[16,24,2048]{2,1,0:T(8,128)(2,1)} async-done(((bf16[16,24,2048]{2,1,0:T(8,128)(2,1)}), bf16[16,24,2048]{2,1,0:T(8,128)(2,1)}, u32[]{:S(2)}, u32[]{:S(2)}) %all-to-all-start.2) | async-done | bytes 1572896 | tf_op jit(solution)/shard_map/all_to_all | solution.py:67
  94.7 3.0 %fusion.1 = bf16[512,1,2048]{2,0,1:T(8,128)(2,1)S(1)} fusion(bf16[384,2048]{1,0:T(8,128)(2,1)} %bitcast.9, f32[384,512]{1,0:T(8,128)} %fusion.7), kind=kOutput, calls=%fused_computation.8 | convolution fusion | flops 808124416 | bytes 4456448 | tf_op jit(solution)/shard_map/dot_general | solution.py:12
  97.7 0.0 all-gather.5.cloned.1.call-done
  97.7 3.7 %fusion.16 = bf16[384,512]{1,0:T(8,128)(2,1)S(1)} fusion(f32[384,512]{1,0:T(8,128)} %fusion.7, bf16[384,2048]{1,0:T(8,128)(2,1)} %bitcast.9, bf16[1,512,2048]{2,1,0:T(8,128)(2,1)} %all-gather.5.cloned.1.call-done), kind=kOutput, calls=%fused_computation.31 | convolution fusion | flops 809238528 | bytes 4849664 | tf_op jit(solution)/shard_map/dot_general | solution.py:18
  101.5 1.3 fusion
  102.8 2.3 %pad_maximum_fusion = bf16[512,2,2048]{2,0,1:T(8,128)(2,1)} fusion(bf16[512,1,2048]{2,0,1:T(8,128)(2,1)S(1)} %fusion.1, bf16[512,1,2048]{2,0,1:T(8,128)(2,1)S(1)} %fusion), kind=kLoop, calls=%fused_computation | loop fusion | flops 2097152 | bytes 8388608 | tf_op jit(solution)/shard_map/stack | solution.py:86
  105.1 0.0 reduce-scatter.2.cloned.1.call-update
  105.1 1.6 copy-done.5
  106.7 2.1 %convolution_convert_fusion.2 = bf16[384,2048]{1,0:T(8,128)(2,1)} fusion(bf16[384,512]{1,0:T(8,128)(2,1)S(1)} %fusion.16, bf16[1,512,2048]{2,1,0:T(8,128)(2,1)S(1)} %copy-done.5), kind=kOutput, calls=%fused_computation.3 | convolution fusion | flops 806092800 | bytes 4063232 | tf_op jit(solution)/shard_map/dot_general | solution.py:72
  108.8 5.0 %all-to-all-start.3 = ((bf16[16,24,2048]{2,1,0:T(8,128)(2,1)}), bf16[16,24,2048]{2,1,0:T(8,128)(2,1)S(1)}, u32[]{:S(2)}, u32[]{:S(2)}) async-start(bf16[16,24,2048]{2,1,0:T(8,128)(2,1)} %bitcast.43), calls=%async_computation.3 | async-start | bytes 3145728 | tf_op jit(solution)/shard_map/all_to_all | solution.py:75
  113.8 3.9 %convolution_convert_fusion.4 = bf16[384,2048]{1,0:T(8,128)(2,1)} fusion(bf16[1,512,2048]{2,1,0:T(8,128)(2,1)} %all-gather.5.cloned.1.call-done, f32[384,512]{1,0:T(8,128)S(1)} %copy-done.6), kind=kOutput, calls=%fused_computation.5 | convolution fusion | flops 807862272 | bytes 4456448 | tf_op jit(solution)/shard_map/dot_general | solution.py:55
  117.7 32.7 %all-to-all-done.3 = bf16[16,24,2048]{2,1,0:T(8,128)(2,1)S(1)} async-done(((bf16[16,24,2048]{2,1,0:T(8,128)(2,1)}), bf16[16,24,2048]{2,1,0:T(8,128)(2,1)S(1)}, u32[]{:S(2)}, u32[]{:S(2)}) %all-to-all-start.3) | async-done | bytes 1572896 | tf_op jit(solution)/shard_map/all_to_all | solution.py:75
  150.4 4.5 %all-to-all-start.1 = ((bf16[16,24,2048]{2,1,0:T(8,128)(2,1)}), bf16[16,24,2048]{2,1,0:T(8,128)(2,1)}, u32[]{:S(2)}, u32[]{:S(2)}) async-start(bf16[16,24,2048]{2,1,0:T(8,128)(2,1)} %bitcast.42), calls=%async_computation.1 | async-start | bytes 3145728 | tf_op jit(solution)/shard_map/all_to_all | solution.py:58
  154.9 1.5 convolution_convert_fusion.6
  156.4 34.8 %all-to-all-done.1 = bf16[16,24,2048]{2,1,0:T(8,128)(2,1)} async-done(((bf16[16,24,2048]{2,1,0:T(8,128)(2,1)}), bf16[16,24,2048]{2,1,0:T(8,128)(2,1)}, u32[]{:S(2)}, u32[]{:S(2)}) %all-to-all-start.1) | async-done | bytes 1572896 | tf_op jit(solution)/shard_map/all_to_all | solution.py:58
  191.2 2.9 %fusion.2 = bf16[192,2048]{1,0:T(8,128)(2,1)} fusion(bf16[384,2048]{1,0:T(8,128)(2,1)} %bitcast.7, f32[192]{0:T(256)S(1)} %bitcast.45, s32[192]{0:T(256)S(1)} %convert_add_fusion), kind=kOutput, calls=%fused_computation.10 | convolution fusion | flops 302850048 | bytes 2360832 | tf_op jit(solution)/shard_map/dot_general | solution.py:12
  194.1 3.1 %slice_bitcast_fusion = (bf16[1,256,2048]{2,1,0:T(8,128)(2,1)}, bf16[1,256,2048]{2,1,0:T(8,128)(2,1)}) fusion(bf16[256,2,2048]{2,0,1:T(8,128)(2,1)} %reduce-scatter.2.cloned.1.call-done), kind=kLoop, calls=%fused_computation.23 | loop fusion | bytes 4194304 | tf_op jit(solution)/shard_map/convert_element_type | solution.py:92
  (13 shorter events, 0.0 us)
Async XLA Ops:
  7.2 1.7 copy-start
  10.6 7.4 %copy-start.3 = (bf16[192,2048]{1,0:T(8,128)(2,1)S(1)}, bf16[192,2048]{1,0:T(8,128)(2,1)}, u32[]{:S(2)}) copy-start(bf16[192,2048]{1,0:T(8,128)(2,1)} %param.9) | copy-start | bytes 2359300
  10.6 7.4 %copy-start.4 = (f32[192,1]{0,1:T(1,128)S(1)}, f32[192,1]{0,1:T(1,128)}, u32[]{:S(2)}) copy-start(f32[192,1]{0,1:T(1,128)} %param.8) | copy-start | bytes 2308
  10.6 43.0 %all-to-all-start = ((bf16[16,24,2048]{2,1,0:T(8,128)(2,1)}), bf16[16,24,2048]{2,1,0:T(8,128)(2,1)S(1)}, u32[]{:S(2)}, u32[]{:S(2)}) async-start(bf16[16,24,2048]{2,1,0:T(8,128)(2,1)} %bitcast.2), calls=%async_computation | async-start | bytes 3145728 | tf_op jit(solution)/shard_map/all_to_all | solution.py:47
  17.3 41.9 %all-gather.3.cloned.1.call-start = ((), (), s32[]{:S(2)}) async-start(), calls=%async_computation.5 | async-start | bytes 3145728 | tf_op jit(solution)/shard_map/all_gather | solution.py:50
  53.6 5.6 %copy-start.1 = (bf16[16,24,2048]{2,1,0:T(8,128)(2,1)}, bf16[16,24,2048]{2,1,0:T(8,128)(2,1)S(1)}, u32[]{:S(2)}) copy-start(bf16[16,24,2048]{2,1,0:T(8,128)(2,1)S(1)} %all-to-all-done) | copy-start | bytes 4718596
  53.6 41.1 %all-to-all-start.2 = ((bf16[16,24,2048]{2,1,0:T(8,128)(2,1)}), bf16[16,24,2048]{2,1,0:T(8,128)(2,1)}, u32[]{:S(2)}, u32[]{:S(2)}) async-start(bf16[16,24,2048]{2,1,0:T(8,128)(2,1)} %bitcast.8), calls=%async_computation.2 | async-start | bytes 3145728 | tf_op jit(solution)/shard_map/all_to_all | solution.py:67
  58.4 39.4 %all-gather.5.cloned.1.call-start = ((), (), s32[]{:S(2)}) async-start(), calls=%async_computation.6 | async-start | bytes 3145728 | tf_op jit(solution)/shard_map/all_gather | solution.py:51
  59.1 135.0 %reduce-scatter.2.cloned.1.call-start = ((), (), s32[]{:S(2)}) async-start(), calls=%async_computation.7 | async-start | bytes 6291456 | tf_op jit(solution)/shard_map/reduce_scatter | solution.py:85
  97.7 3.7 %copy-start.2 = (bf16[16,24,2048]{2,1,0:T(8,128)(2,1)S(1)}, bf16[16,24,2048]{2,1,0:T(8,128)(2,1)}, u32[]{:S(2)}) copy-start(bf16[16,24,2048]{2,1,0:T(8,128)(2,1)} %copy-done.1) | copy-start | bytes 4718596
  105.1 1.6 copy-start.5
  108.8 5.0 %copy-start.6 = (f32[384,512]{1,0:T(8,128)S(1)}, f32[384,512]{1,0:T(8,128)}, u32[]{:S(2)}) copy-start(f32[384,512]{1,0:T(8,128)} %fusion.7) | copy-start | bytes 2359300
  108.8 41.6 %all-to-all-start.3 = ((bf16[16,24,2048]{2,1,0:T(8,128)(2,1)}), bf16[16,24,2048]{2,1,0:T(8,128)(2,1)S(1)}, u32[]{:S(2)}, u32[]{:S(2)}) async-start(bf16[16,24,2048]{2,1,0:T(8,128)(2,1)} %bitcast.43), calls=%async_computation.3 | async-start | bytes 3145728 | tf_op jit(solution)/shard_map/all_to_all | solution.py:75
  150.4 40.8 %all-to-all-start.1 = ((bf16[16,24,2048]{2,1,0:T(8,128)(2,1)}), bf16[16,24,2048]{2,1,0:T(8,128)(2,1)}, u32[]{:S(2)}, u32[]{:S(2)}) async-start(bf16[16,24,2048]{2,1,0:T(8,128)(2,1)} %bitcast.42), calls=%async_computation.1 | async-start | bytes 3145728 | tf_op jit(solution)/shard_map/all_to_all | solution.py:58
Sparse Core Ops, SparseCore 0:
  19.6 33.7 all-gather.2
  60.7 33.7 all-gather.4
  105.2 53.7 reduce-scatter.1
where the time goes:
time: 204 us
  waiting for transfers between devices  135 us (66%)
  matrix products  26.5 us (13%)
  starting transfers between devices  21.1 us (10%)
  between operations  13.8 us (7%)
  local copies, waits for them, and re-layouts  4.7 us (2%)
  other arithmetic  3.02 us (1%)
    all_to_all x1, waiting for transfers between devices, per_device(): lax.all_to_all(expert_out.reshape(n_expert, capacity, width), 'expert', s...  34.8 us
    all_to_all x1, waiting for transfers between devices, per_device(): lax.all_to_all(place(tokens), 'expert', split_axis=0, concat_axis=0, tile...  33.8 us
    all_to_all x1, waiting for transfers between devices, per_device(): lax.all_to_all(slot_grad.reshape(n_expert, capacity, width), 'expert', sp...  32.7 us
    all_to_all x1, waiting for transfers between devices, per_device(): lax.all_to_all(place(scaled), 'expert', split_axis=0, concat_axis=0, tile...  32 us
    dot_general x4, matrix products, contract_rows(): lax.dot_general(left, right, (((0,), (0,)), ((), ())), preferred_element_...  8.72 us
    dot_general x2, matrix products, contract_cols(): lax.dot_general(left, right, (((1,), (1,)), ((), ())), preferred_element_...  7.22 us
    all_to_all x1, starting transfers between devices, per_device(): lax.all_to_all(place(tokens), 'expert', split_axis=0, concat_axis=0, tile...  6.69 us
    all_to_all x1, starting transfers between devices, per_device(): lax.all_to_all(slot_grad.reshape(n_expert, capacity, width), 'expert', sp...  5.01 us
  transfers between devices with their start and end apart: 7, of which 4 were waited for; matrix products, arithmetic and copies ran while one was open for 9% of the time, Pallas kernels for 0%

commit v1 on v0

v1 whole, which is shorter than its diff:
```python
import functools

import jax
import jax.numpy as jnp
from jax import lax
from jax.experimental import pallas as pl
from jax.experimental.pallas import tpu as pltpu
from jax.sharding import PartitionSpec as P

MESH = pl.DeviceIdType.MESH
GROUPS = 4
UP, DOWN, TERM_DOWN, TERM_UP = range(4)
TOK, COT, OUT, GRAD = range(4)


def smooth(values):
    return jax.nn.gelu(values, approximate=True)


def dot_nt(left, right):
    return lax.dot_general(
        left, right, (((1,), (1,)), ((), ())), preferred_element_type=jnp.float32
    )


def dot_nn(left, right):
    return jnp.dot(left, right, preferred_element_type=jnp.float32)


def expert_kernel(
    n_dp, n, tok_ref, cot_ref, up_ref, down_ref,
    ret_out, ret_grad, gup_ref, gdown_ref,
    arr_tok, arr_cot, x_all, c_all, up_all, down_all, preact_all, hid_all, pg_all,
    left_t, out_buf, grad_buf, terms, landed, send_sem, recv_sem, dsend_sem, drecv_sem, local_sem,
):
    me = lax.axis_index("expert")
    mydp = lax.axis_index("dp")
    cap, width = tok_ref.shape[1], tok_ref.shape[2]
    ff = hid_all.shape[1]
    share = ff // n_dp
    slots = n // GROUPS
    rows = slots * cap

    def offset(i):
        return n // 2 + (i // 2) * (2 * (i % 2) - 1)

    def target(i):
        return lax.rem(me + offset(i), n)

    def origin(i):
        return lax.rem(me - offset(i) + n, n)

    def dispatch(stream, src, dst, i):
        peer = target(i)
        return pltpu.make_async_remote_copy(
            src_ref=src.at[peer], dst_ref=dst.at[i],
            send_sem=send_sem.at[stream, i], recv_sem=recv_sem.at[stream, i],
            device_id=(mydp, peer), device_id_type=MESH,
        )

    def give_back(stream, src, dst, i):
        peer = origin(i)
        return pltpu.make_async_remote_copy(
            src_ref=src.at[i], dst_ref=dst.at[me],
            send_sem=send_sem.at[stream, i], recv_sem=recv_sem.at[stream, i],
            device_id=(mydp, peer), device_id_type=MESH,
        )

    def dp_peer(j):
        return lax.rem(mydp + j, n_dp)

    def gather(which, src, dst, j):
        return pltpu.make_async_remote_copy(
            src_ref=src.at[0], dst_ref=dst.at[mydp],
            send_sem=dsend_sem.at[which, j], recv_sem=drecv_sem.at[which, j],
            device_id=(dp_peer(j), me), device_id_type=MESH,
        )

    def swap(which, j):
        return pltpu.make_async_remote_copy(
            src_ref=terms.at[which - TERM_DOWN, dp_peer(j)],
            dst_ref=landed.at[which - TERM_DOWN, j - 1],
            send_sem=dsend_sem.at[which, j], recv_sem=drecv_sem.at[which, j],
            device_id=(dp_peer(j), me), device_id_type=MESH,
        )

    def each(low, high, body):
        lax.fori_loop(low, high, lambda i, c: (body(i), c)[1], 0)

    own = [
        pltpu.make_async_copy(tok_ref.at[me], arr_tok.at[0], local_sem.at[0]),
        pltpu.make_async_copy(cot_ref.at[me], arr_cot.at[0], local_sem.at[1]),
        pltpu.make_async_copy(up_ref.at[0], up_all.at[mydp], local_sem.at[2]),
        pltpu.make_async_copy(down_ref.at[0], down_all.at[mydp], local_sem.at[3]),
    ]
    for copy in own:
        copy.start()

    barrier = pltpu.get_barrier_semaphore()
    each(1, n, lambda i: pl.semaphore_signal(
        barrier, inc=1, device_id=(mydp, target(i)), device_id_type=MESH))
    each(1, n_dp, lambda j: pl.semaphore_signal(
        barrier, inc=1, device_id=(dp_peer(j), me), device_id_type=MESH))
    pl.semaphore_wait(barrier, n - 1 + n_dp - 1)

    each(1, n_dp, lambda j: gather(UP, up_ref, up_all, j).start())
    each(1, n, lambda i: dispatch(TOK, tok_ref, arr_tok, i).start())
    each(1, n_dp, lambda j: gather(DOWN, down_ref, down_all, j).start())
    each(1, n, lambda i: dispatch(COT, cot_ref, arr_cot, i).start())

    for copy in own:
        copy.wait()
    each(1, n_dp, lambda j: gather(UP, up_ref, up_all, j).wait_recv())

    def take(arrived, g):
        block = arrived[pl.ds(g * slots, slots)].astype(jnp.float32)
        return block.reshape(rows, width).astype(jnp.bfloat16)

    def put(buffer, g, values):
        buffer[pl.ds(g * slots, slots)] = values.reshape(slots, cap, width).astype(jnp.bfloat16)

    def span(g):
        return pl.ds(pl.multiple_of(g * rows, rows), rows)

    def first(g):
        return jnp.where(g == 0, 1, g * slots)

    def forward(g):
        each(first(g), (g + 1) * slots, lambda i: dispatch(TOK, tok_ref, arr_tok, i).wait_recv())
        x = take(arr_tok, g)
        x_all[span(g)] = x
        preact = dot_nt(x, up_all[...].reshape(ff, width))
        preact_all[span(g)] = preact
        hidden = smooth(preact).astype(jnp.bfloat16)
        hid_all[span(g)] = hidden

    def forward_out(g):
        put(out_buf, g, dot_nn(hid_all[span(g)], down_all[...].reshape(ff, width)))
        each(first(g), (g + 1) * slots, lambda i: give_back(OUT, out_buf, ret_out, i).start())

    def backward(g):
        each(first(g), (g + 1) * slots, lambda i: dispatch(COT, cot_ref, arr_cot, i).wait_recv())
        c = take(arr_cot, g)
        c_all[span(g)] = c
        hidden_grad = dot_nt(c, down_all[...].reshape(ff, width))
        unused, pull = jax.vjp(smooth, preact_all[span(g)])
        preact_grad = pull(hidden_grad)[0].astype(jnp.bfloat16)
        pg_all[span(g)] = preact_grad
        put(grad_buf, g, dot_nn(preact_grad, up_all[...].reshape(ff, width)))
        each(first(g), (g + 1) * slots, lambda i: give_back(GRAD, grad_buf, ret_grad, i).start())

    each(0, GROUPS, forward)
    each(1, n_dp, lambda j: gather(DOWN, down_ref, down_all, j).wait_recv())
    each(0, GROUPS, forward_out)
    own_out = pltpu.make_async_copy(out_buf.at[0], ret_out.at[me], local_sem.at[0])
    own_out.start()
    each(0, GROUPS, backward)
    own_grad = pltpu.make_async_copy(grad_buf.at[0], ret_grad.at[me], local_sem.at[1])
    own_grad.start()

    def weight_terms(which, left, right):
        left_t[...] = left[...].astype(jnp.float32).T.astype(jnp.bfloat16)

        def one(j):
            q = dp_peer(j)
            block = left_t[pl.ds(pl.multiple_of(q * share, share), share)]
            terms[which - TERM_DOWN, q] = dot_nn(block, right[...]).astype(jnp.bfloat16)

        def send(j):
            one(j)
            swap(which, j).start()

        each(1, n_dp, send)
        one(0)

    def total(which, dest):
        each(1, n_dp, lambda j: swap(which, j).wait_recv())
        result = terms[which - TERM_DOWN, mydp].astype(jnp.float32)
        for j in range(1, n_dp):
            result = result + landed[which - TERM_DOWN, j - 1].astype(jnp.float32)
        dest[0] = result.astype(jnp.bfloat16)

    weight_terms(TERM_DOWN, hid_all, c_all)
    weight_terms(TERM_UP, pg_all, x_all)
    total(TERM_DOWN, gdown_ref)
    total(TERM_UP, gup_ref)

    own_out.wait()
    own_grad.wait()
    each(1, n, lambda i: give_back(OUT, out_buf, ret_out, i).wait_recv())
    each(1, n, lambda i: give_back(GRAD, grad_buf, ret_grad, i).wait_recv())

    def sent(i):
        dispatch(TOK, tok_ref, arr_tok, i).wait_send()
        dispatch(COT, cot_ref, arr_cot, i).wait_send()
        give_back(OUT, out_buf, ret_out, i).wait_send()
        give_back(GRAD, grad_buf, ret_grad, i).wait_send()

    each(1, n, sent)

    def dp_sent(j):
        gather(UP, up_ref, up_all, j).wait_send()
        gather(DOWN, down_ref, down_all, j).wait_send()
        swap(TERM_DOWN, j).wait_send()
        swap(TERM_UP, j).wait_send()

    each(1, n_dp, dp_sent)


def expert_call(tok, cot, up, down):
    n_dp, n = lax.axis_size("dp"), lax.axis_size("expert")
    cap, width = tok.shape[1], tok.shape[2]
    share = up.shape[1]
    ff, slot_total = share * n_dp, n * cap
    slab = jax.ShapeDtypeStruct((n, cap, width), jnp.bfloat16)
    weight = jax.ShapeDtypeStruct((1, share, width), jnp.bfloat16)
    hbm, vmem = pl.BlockSpec(memory_space=pl.ANY), pl.BlockSpec(memory_space=pltpu.VMEM)

    def half(*dims):
        return pltpu.VMEM(dims, jnp.bfloat16)

    return pl.pallas_call(
        functools.partial(expert_kernel, n_dp, n),
        out_shape=(slab, slab, weight, weight),
        in_specs=[hbm] * 4,
        out_specs=(hbm, hbm, vmem, vmem),
        scratch_shapes=[
            half(n, cap, width), half(n, cap, width),
            half(slot_total, width), half(slot_total, width),
            half(n_dp, share, width), half(n_dp, share, width),
            pltpu.VMEM((slot_total, ff), jnp.float32),
            half(slot_total, ff), half(slot_total, ff),
            half(ff, slot_total),
            half(n, cap, width), half(n, cap, width),
            half(2, n_dp, share, width), half(2, n_dp - 1, share, width),
            pltpu.SemaphoreType.DMA((4, n)), pltpu.SemaphoreType.DMA((4, n)),
            pltpu.SemaphoreType.DMA((4, n_dp)), pltpu.SemaphoreType.DMA((4, n_dp)),
            pltpu.SemaphoreType.DMA((4,)),
        ],
        compiler_params=pltpu.CompilerParams(
            collective_id=0, has_side_effects=True, vmem_limit_bytes=48 * 1024 * 1024
        ),
        cost_estimate=pl.CostEstimate(
            flops=12 * slot_total * width * ff, bytes_accessed=8 * slot_total * width,
            transcendentals=2 * slot_total * ff,
        ),
    )(tok, cot, up, down)


def contract_rows(left, right):
    return lax.dot_general(
        left, right, (((0,), (0,)), ((), ())), preferred_element_type=jnp.float32
    )


def per_device(tokens, routing, gate_scale, cotangent, up_weight, down_weight):
    tok_count, width = tokens.shape
    n_expert = lax.axis_size("expert")
    capacity = 2 * tok_count // n_expert
    capacity = -(-capacity // 8) * 8
    slot_total = n_expert * capacity
    ids = routing[:, 0]
    onehot = (ids[:, None] == jnp.arange(n_expert, dtype=jnp.int32)[None, :]).astype(jnp.float32)
    position = jnp.arange(tok_count, dtype=jnp.int32)
    lower_tri = (position[:, None] >= position[None, :]).astype(jnp.float32)
    counts = jnp.dot(
        lower_tri, onehot, precision=lax.Precision.HIGHEST, preferred_element_type=jnp.float32
    )
    slot_rank = (jnp.sum(counts * onehot, axis=1) - 1.0).astype(jnp.int32)
    slot_index = ids * capacity + slot_rank
    placer = (jnp.arange(slot_total, dtype=jnp.int32)[:, None] == slot_index[None, :]).astype(
        jnp.bfloat16
    )

    def place(values):
        placed = jnp.dot(placer, values, preferred_element_type=jnp.float32).astype(jnp.bfloat16)
        return placed.reshape(n_expert, capacity, width)

    scaled = (gate_scale * cotangent.astype(jnp.float32)).astype(jnp.bfloat16)
    returned, grad_back, grad_up, grad_down = expert_call(
        place(tokens), place(scaled), up_weight, down_weight
    )
    picked = contract_rows(placer, returned.reshape(slot_total, width))
    output_rows = (gate_scale * picked).astype(jnp.bfloat16)
    token_grad = contract_rows(placer, grad_back.reshape(slot_total, width)).astype(jnp.bfloat16)
    return (output_rows, token_grad, grad_up, grad_down)


def solution(mesh):
    tokens, experts = P(("dp", "expert"), None), P("expert", "dp", None)
    return jax.shard_map(
        per_device,
        mesh=mesh,
        in_specs=(tokens, tokens, tokens, tokens, experts, experts),
        out_specs=(tokens, tokens, experts, experts),
        check_vma=False,
    )
```

time: 204 us -> 170 us (0.83)
  Pallas kernels: 0 us -> 157 us
  waiting for transfers between devices: 135 us -> 0 us
  starting transfers between devices: 21.1 us -> 0 us
  matrix products: 26.5 us -> 8.62 us
  between operations: 13.8 us -> 0.67 us
  local copies, waits for them, and re-layouts: 4.7 us -> 1.96 us
  other arithmetic: 3.02 us -> 0.7 us
    pallas_call x0 -> x1, Pallas kernels: none -> 157 us  [expert_call(): pl.pallas_call(functools.partial(expert_kernel, n_dp, n), out_shape=(slab...]
    all_to_all x4 -> x0, waiting for transfers between devices: 133 us -> none  [the longest x1 34.8 us: per_device(): lax.all_to_all(expert_out.reshape(n_expert, capacity, width), 'expert', s...]
    all_to_all x4 -> x0, starting transfers between devices: 21 us -> none  [the longest x1 6.69 us: per_device(): lax.all_to_all(place(tokens), 'expert', split_axis=0, concat_axis=0, tile...]
    dot_general x4 -> x0, matrix products: 13.3 us -> none  [the longest x2 7.22 us: contract_cols(): lax.dot_general(left, right, (((1,), (1,)), ((), ())), preferred_element_...]
    dot_general x4 -> x2, matrix products: 8.72 us -> 3.01 us  [contract_rows(): lax.dot_general(left, right, (((0,), (0,)), ((), ())), preferred_element_...]
    convert_element_type x1 -> x0, local copies, waits for them, and re-layouts: 3.1 us -> none  [per_device(): grad_down = summed_terms[:, 1, :].astype(jnp.bfloat16)[None]]
    another operation x1 -> x0, other arithmetic: 2.32 us -> none  [per_device(): jnp.stack((term_up, term_down), axis=1).astype(jnp.bfloat16)]
  transfers between devices with their start and end apart: 7 -> 0, of which waited for: 4 -> 0; matrix products, arithmetic and copies ran while one was open for 9% -> 0% of each run, Pallas kernels for 0% -> 0%
where the time goes in v1:
time: 170 us; the launch traced here: 169 us
  Pallas kernels  157 us (92%)
  matrix products  8.62 us (5%)
  local copies, waits for them, and re-layouts  1.96 us (1%)
    pallas_call x1, Pallas kernels, expert_call(): pl.pallas_call(functools.partial(expert_kernel, n_dp, n), out_shape=(slab...  157 us
    dot_general x2, matrix products, place(): jnp.dot(placer, values, preferred_element_type=jnp.float32)  4.68 us

profile of v1, /device:TPU:11, one launch (start us, length us, event | category | flops | bytes accessed | tf_op | source)
XLA Modules:
  0.0 168.6 jit_solution(791988337263514602)
XLA Ops:
  0.6 0.0 copy-start
  0.6 0.9 fusion.1
  1.6 0.7 convert_add_fusion
  2.3 2.9 %convolution_convert_fusion = bf16[384,2048]{1,0:T(8,128)(2,1)} fusion(bf16[192,2048]{1,0:T(8,128)(2,1)} %param.9, f32[192]{0:T(256)} %bitcast.13, s32[192]{0:T(256)S(1)} %convert_add_fusion), kind=kOutput, calls=%fused_computation | convolution fusion | flops 304029696 | bytes 2360832 | tf_op jit(solution)/shard_map/dot_general | solution.py:276
  5.2 0.0 copy-start.1
  5.2 0.0 copy-start.2
  5.2 0.0 copy-done
  5.2 1.7 %convolution_convert_fusion.1 = bf16[384,2048]{1,0:T(8,128)(2,1)} fusion(bf16[192,2048]{1,0:T(8,128)(2,1)S(1)} %copy-done, s32[192]{0:T(256)S(1)} %convert_add_fusion), kind=kOutput, calls=%fused_computation.1 | convolution fusion | flops 302850048 | bytes 2360064 | tf_op jit(solution)/shard_map/dot_general | solution.py:276
  7.0 0.0 copy-done.1
  7.0 0.0 copy-done.2
  7.0 0.0 copy-start.4
  7.0 156.7 %shard_map.93 = (bf16[16,24,2048]{2,1,0:T(8,128)(2,1)S(1)}, bf16[16,24,2048]{2,1,0:T(8,128)(2,1)}, bf16[1,256,2048]{2,1,0:T(8,128)(2,1)S(1)}, bf16[1,256,2048]{2,1,0:T(8,128)(2,1)S(1)}) custom-call(bf16[16,24,2048]{2,1,0:T(8,128)(2,1)} %bitcast.11, bf16[16,24,2048]{2,1,0:T(8,128)(2,1)} %bitcast.12, bf16[1,256,2048]{2,1,0:T(8,128)(2,1)S(1)} %copy-done.1, ...), custom_call_target="tpu_custom_call" | custom-call | flops 4831838208 | bytes 6291456 | tf_op jit(solution)/shard_map/pallas_call | solution.py:222
  163.6 0.0 copy-start.3
  163.7 0.0 copy-done.4
  163.7 1.5 fusion
  165.2 0.0 copy-done.3
  165.2 1.5 convolution_convert_fusion.2
  166.7 1.0 copy.12
  167.7 1.0 copy.13
Async XLA Ops:
  0.6 4.6 %copy-start = (bf16[192,2048]{1,0:T(8,128)(2,1)S(1)}, bf16[192,2048]{1,0:T(8,128)(2,1)}, u32[]{:S(2)}) copy-start(bf16[192,2048]{1,0:T(8,128)(2,1)} %param.6) | copy-start | bytes 2359300
  5.2 1.7 %copy-start.1 = (bf16[1,256,2048]{2,1,0:T(8,128)(2,1)S(1)}, bf16[1,256,2048]{2,1,0:T(8,128)(2,1)}, u32[]{:S(2)}) copy-start(bf16[1,256,2048]{2,1,0:T(8,128)(2,1)} %up_ref.1) | copy-start | bytes 3145732
  5.2 1.7 %copy-start.2 = (bf16[1,256,2048]{2,1,0:T(8,128)(2,1)S(1)}, bf16[1,256,2048]{2,1,0:T(8,128)(2,1)}, u32[]{:S(2)}) copy-start(bf16[1,256,2048]{2,1,0:T(8,128)(2,1)} %down_ref.1) | copy-start | bytes 3145732
  7.0 156.7 %copy-start.4 = (f32[192,1]{0,1:T(1,128)S(1)}, f32[192,1]{0,1:T(1,128)}, u32[]{:S(2)}) copy-start(f32[192,1]{0,1:T(1,128)} %param.8) | copy-start | bytes 2308
  163.6 1.5 copy-start.3

commit v2 on v1

--- a/solution.py
+++ b/solution.py
@@ -9,6 +9,7 @@
 
 MESH = pl.DeviceIdType.MESH
 GROUPS = 4
+PLACE_BLOCKS = 4
 UP, DOWN, TERM_DOWN, TERM_UP = range(4)
 TOK, COT, OUT, GRAD = range(4)
 
@@ -28,14 +29,14 @@
 
 
 def expert_kernel(
-    n_dp, n, tok_ref, cot_ref, up_ref, down_ref,
-    ret_out, ret_grad, gup_ref, gdown_ref,
-    arr_tok, arr_cot, x_all, c_all, up_all, down_all, preact_all, hid_all, pg_all,
-    left_t, out_buf, grad_buf, terms, landed, send_sem, recv_sem, dsend_sem, drecv_sem, local_sem,
+    n_dp, n, cap, ids_ref, gate_ref, tokens_hbm, cotangent_hbm, up_ref, down_ref,
+    ret_out, ret_grad, gup_ref, gdown_ref, index_ref,
+    tokens_ref, cotangent_ref, tok_ref, cot_ref, arr_tok, arr_cot, x_all, c_all, up_all, down_all, preact_all, hid_all, pg_all,
+    placer_ref, left_t, out_buf, grad_buf, terms, landed, send_sem, recv_sem, dsend_sem, drecv_sem, local_sem,
 ):
     me = lax.axis_index("expert")
     mydp = lax.axis_index("dp")
-    cap, width = tok_ref.shape[1], tok_ref.shape[2]
+    count, width = tokens_ref.shape
     ff = hid_all.shape[1]
     share = ff // n_dp
     slots = n // GROUPS
@@ -87,13 +88,15 @@
     def each(low, high, body):
         lax.fori_loop(low, high, lambda i, c: (body(i), c)[1], 0)
 
+    own_tok = pltpu.make_async_copy(tok_ref.at[me], arr_tok.at[0], local_sem.at[0])
+    own_cot = pltpu.make_async_copy(cot_ref.at[me], arr_cot.at[0], local_sem.at[1])
     own = [
-        pltpu.make_async_copy(tok_ref.at[me], arr_tok.at[0], local_sem.at[0]),
-        pltpu.make_async_copy(cot_ref.at[me], arr_cot.at[0], local_sem.at[1]),
         pltpu.make_async_copy(up_ref.at[0], up_all.at[mydp], local_sem.at[2]),
         pltpu.make_async_copy(down_ref.at[0], down_all.at[mydp], local_sem.at[3]),
     ]
-    for copy in own:
+    load_tok = pltpu.make_async_copy(tokens_hbm, tokens_ref, local_sem.at[4])
+    load_cot = pltpu.make_async_copy(cotangent_hbm, cotangent_ref, local_sem.at[5])
+    for copy in [load_tok, load_cot] + own:
         copy.start()
 
     barrier = pltpu.get_barrier_semaphore()
@@ -101,13 +104,50 @@
         barrier, inc=1, device_id=(mydp, target(i)), device_id_type=MESH))
     each(1, n_dp, lambda j: pl.semaphore_signal(
         barrier, inc=1, device_id=(dp_peer(j), me), device_id_type=MESH))
+
+    ids = ids_ref[...]
+    onehot = ids == lax.broadcasted_iota(jnp.int32, (n, count), 0)
+    earlier = lax.broadcasted_iota(jnp.int32, (count, count), 0) < lax.broadcasted_iota(
+        jnp.int32, (count, count), 1
+    )
+    ranks = dot_nn(
+        onehot.astype(jnp.float32).astype(jnp.bfloat16),
+        earlier.astype(jnp.float32).astype(jnp.bfloat16),
+    )
+    rank = jnp.sum(jnp.where(onehot, ranks, 0.0), axis=0, keepdims=True)
+    index = ids * cap + rank.astype(jnp.int32)
+    index_ref[...] = index
+    placer_ref[...] = (
+        (lax.broadcasted_iota(jnp.int32, (n * cap, count), 0) == index)
+        .astype(jnp.float32)
+        .astype(jnp.bfloat16)
+    )
+    block = width // PLACE_BLOCKS
+
+    def place_tok(b):
+        columns = pl.ds(pl.multiple_of(b * block, block), block)
+        placed = dot_nn(placer_ref[...], tokens_ref[:, columns])
+        tok_ref[:, :, columns] = placed.reshape(n, cap, block).astype(jnp.bfloat16)
+
+    def place_cot(b):
+        columns = pl.ds(pl.multiple_of(b * block, block), block)
+        scaled = gate_ref[...] * cotangent_ref[:, columns].astype(jnp.float32)
+        placed = dot_nn(placer_ref[...], scaled.astype(jnp.bfloat16))
+        cot_ref[:, :, columns] = placed.reshape(n, cap, block).astype(jnp.bfloat16)
+
+    load_tok.wait()
+    each(0, PLACE_BLOCKS, place_tok)
+    own_tok.start()
     pl.semaphore_wait(barrier, n - 1 + n_dp - 1)
 
+    each(1, n, lambda i: dispatch(TOK, tok_ref, arr_tok, i).start())
     each(1, n_dp, lambda j: gather(UP, up_ref, up_all, j).start())
-    each(1, n, lambda i: dispatch(TOK, tok_ref, arr_tok, i).start())
     each(1, n_dp, lambda j: gather(DOWN, down_ref, down_all, j).start())
-    each(1, n, lambda i: dispatch(COT, cot_ref, arr_cot, i).start())
-
+    load_cot.wait()
+    each(0, PLACE_BLOCKS, place_cot)
+    own_cot.start()
+
+    own_tok.wait()
     for copy in own:
         copy.wait()
     each(1, n_dp, lambda j: gather(UP, up_ref, up_all, j).wait_recv())
@@ -126,20 +166,20 @@
         return jnp.where(g == 0, 1, g * slots)
 
     def forward(g):
-        each(first(g), (g + 1) * slots, lambda i: dispatch(TOK, tok_ref, arr_tok, i).wait_recv())
+        low, high = first(g), (g + 1) * slots
+        each(low, high, lambda i: dispatch(TOK, tok_ref, arr_tok, i).wait_recv())
+        each(low, high, lambda i: dispatch(COT, cot_ref, arr_cot, i).start())
         x = take(arr_tok, g)
         x_all[span(g)] = x
         preact = dot_nt(x, up_all[...].reshape(ff, width))
         preact_all[span(g)] = preact
-        hidden = smooth(preact).astype(jnp.bfloat16)
-        hid_all[span(g)] = hidden
-
-    def forward_out(g):
+        hid_all[span(g)] = smooth(preact).astype(jnp.bfloat16)
+
+    def backward(g):
+        low, high = first(g), (g + 1) * slots
         put(out_buf, g, dot_nn(hid_all[span(g)], down_all[...].reshape(ff, width)))
-        each(first(g), (g + 1) * slots, lambda i: give_back(OUT, out_buf, ret_out, i).start())
-
-    def backward(g):
-        each(first(g), (g + 1) * slots, lambda i: dispatch(COT, cot_ref, arr_cot, i).wait_recv())
+        each(low, high, lambda i: dispatch(COT, cot_ref, arr_cot, i).wait_recv())
+        each(low, high, lambda i: give_back(OUT, out_buf, ret_out, i).start())
         c = take(arr_cot, g)
         c_all[span(g)] = c
         hidden_grad = dot_nt(c, down_all[...].reshape(ff, width))
@@ -147,14 +187,14 @@
         preact_grad = pull(hidden_grad)[0].astype(jnp.bfloat16)
         pg_all[span(g)] = preact_grad
         put(grad_buf, g, dot_nn(preact_grad, up_all[...].reshape(ff, width)))
-        each(first(g), (g + 1) * slots, lambda i: give_back(GRAD, grad_buf, ret_grad, i).start())
+        each(low, high, lambda i: give_back(GRAD, grad_buf, ret_grad, i).start())
 
     each(0, GROUPS, forward)
+    own_cot.wait()
     each(1, n_dp, lambda j: gather(DOWN, down_ref, down_all, j).wait_recv())
-    each(0, GROUPS, forward_out)
+    each(0, GROUPS, backward)
     own_out = pltpu.make_async_copy(out_buf.at[0], ret_out.at[me], local_sem.at[0])
     own_out.start()
-    each(0, GROUPS, backward)
     own_grad = pltpu.make_async_copy(grad_buf.at[0], ret_grad.at[me], local_sem.at[1])
     own_grad.start()
 
@@ -207,9 +247,9 @@
     each(1, n_dp, dp_sent)
 
 
-def expert_call(tok, cot, up, down):
+def expert_call(cap, ids, gate, tok, cot, up, down):
     n_dp, n = lax.axis_size("dp"), lax.axis_size("expert")
-    cap, width = tok.shape[1], tok.shape[2]
+    count, width = tok.shape
     share = up.shape[1]
     ff, slot_total = share * n_dp, n * cap
     slab = jax.ShapeDtypeStruct((n, cap, width), jnp.bfloat16)
@@ -220,31 +260,33 @@
         return pltpu.VMEM(dims, jnp.bfloat16)
 
     return pl.pallas_call(
-        functools.partial(expert_kernel, n_dp, n),
-        out_shape=(slab, slab, weight, weight),
-        in_specs=[hbm] * 4,
-        out_specs=(hbm, hbm, vmem, vmem),
+        functools.partial(expert_kernel, n_dp, n, cap),
+        out_shape=(slab, slab, weight, weight, jax.ShapeDtypeStruct((1, count), jnp.int32)),
+        in_specs=[vmem] * 2 + [hbm] * 4,
+        out_specs=(hbm, hbm, vmem, vmem, vmem),
         scratch_shapes=[
+            half(count, width), half(count, width),
+            half(n, cap, width), half(n, cap, width),
             half(n, cap, width), half(n, cap, width),
             half(slot_total, width), half(slot_total, width),
             half(n_dp, share, width), half(n_dp, share, width),
             pltpu.VMEM((slot_total, ff), jnp.float32),
             half(slot_total, ff), half(slot_total, ff),
-            half(ff, slot_total),
+            half(slot_total, count), half(ff, slot_total),
             half(n, cap, width), half(n, cap, width),
             half(2, n_dp, share, width), half(2, n_dp - 1, share, width),
             pltpu.SemaphoreType.DMA((4, n)), pltpu.SemaphoreType.DMA((4, n)),
             pltpu.SemaphoreType.DMA((4, n_dp)), pltpu.SemaphoreType.DMA((4, n_dp)),
-            pltpu.SemaphoreType.DMA((4,)),
+            pltpu.SemaphoreType.DMA((6,)),
         ],
         compiler_params=pltpu.CompilerParams(
-            collective_id=0, has_side_effects=True, vmem_limit_bytes=48 * 1024 * 1024
+            collective_id=0, has_side_effects=True, vmem_limit_bytes=60 * 1024 * 1024
         ),
         cost_estimate=pl.CostEstimate(
             flops=12 * slot_total * width * ff, bytes_accessed=8 * slot_total * width,
             transcendentals=2 * slot_total * ff,
         ),
-    )(tok, cot, up, down)
+    )(ids, gate, tok, cot, up, down)
 
 
 def contract_rows(left, right):
@@ -259,27 +301,10 @@
     capacity = 2 * tok_count // n_expert
     capacity = -(-capacity // 8) * 8
     slot_total = n_expert * capacity
-    ids = routing[:, 0]
-    onehot = (ids[:, None] == jnp.arange(n_expert, dtype=jnp.int32)[None, :]).astype(jnp.float32)
-    position = jnp.arange(tok_count, dtype=jnp.int32)
-    lower_tri = (position[:, None] >= position[None, :]).astype(jnp.float32)
-    counts = jnp.dot(
-        lower_tri, onehot, precision=lax.Precision.HIGHEST, preferred_element_type=jnp.float32
-    )
-    slot_rank = (jnp.sum(counts * onehot, axis=1) - 1.0).astype(jnp.int32)
-    slot_index = ids * capacity + slot_rank
-    placer = (jnp.arange(slot_total, dtype=jnp.int32)[:, None] == slot_index[None, :]).astype(
-        jnp.bfloat16
-    )
-
-    def place(values):
-        placed = jnp.dot(placer, values, preferred_element_type=jnp.float32).astype(jnp.bfloat16)
-        return placed.reshape(n_expert, capacity, width)
-
-    scaled = (gate_scale * cotangent.astype(jnp.float32)).astype(jnp.bfloat16)
-    returned, grad_back, grad_up, grad_down = expert_call(
-        place(tokens), place(scaled), up_weight, down_weight
-    )
+    returned, grad_back, grad_up, grad_down, slot_index = expert_call(
+        capacity, routing.reshape(1, tok_count), gate_scale, tokens, cotangent, up_weight, down_weight
+    )
+    placer = (jnp.arange(slot_total, dtype=jnp.int32)[:, None] == slot_index).astype(jnp.bfloat16)
     picked = contract_rows(placer, returned.reshape(slot_total, width))
     output_rows = (gate_scale * picked).astype(jnp.bfloat16)
     token_grad = contract_rows(placer, grad_back.reshape(slot_total, width)).astype(jnp.bfloat16)

time: 170 us -> 166 us (0.976)
  matrix products: 8.62 us -> 4.54 us
  local copies, waits for them, and re-layouts: 1.96 us -> 4.03 us
    dot_general x3 -> x0, matrix products: 5.61 us -> none  [the longest x2 4.68 us: place(): jnp.dot(placer, values, preferred_element_type=jnp.float32)]
    unnamed x12 -> x13, local copies, waits for them, and re-layouts: 1.96 us -> 4.03 us
where the time goes in v2:
time: 166 us
  Pallas kernels  157 us (95%)
  matrix products  4.54 us (3%)
  local copies, waits for them, and re-layouts  4.03 us (2%)
    pallas_call x1, Pallas kernels, expert_call(): pl.pallas_call(functools.partial(expert_kernel, n_dp, n, cap), out_shape=...  157 us
    dot_general x2, matrix products, contract_rows(): lax.dot_general(left, right, (((0,), (0,)), ((), ())), preferred_element_...  4.54 us
    unnamed x13, local copies, waits for them, and re-layouts  4.03 us

profile of v2, /device:TPU:11, one launch (start us, length us, event | category | flops | bytes accessed | tf_op | source)
XLA Modules:
  0.0 165.8 jit_solution(14761635263115776830)
XLA Ops:
  0.6 1.4 copy.10.gate_ref
  2.1 156.6 %shard_map.93 = (bf16[16,24,2048]{2,1,0:T(8,128)(2,1)}, bf16[16,24,2048]{2,1,0:T(8,128)(2,1)}, bf16[1,256,2048]{2,1,0:T(8,128)(2,1)}, bf16[1,256,2048]{2,1,0:T(8,128)(2,1)}, s32[1,192]{1,0:T(1,128)}) custom-call(s32[1,192]{1,0:T(1,128)} %bitcast.12, f32[192,1]{1,0:T(8,128)} %copy.10.gate_ref, bf16[192,2048]{1,0:T(8,128)(2,1)} %tokens_hbm.1, ...), custom_call_target="tpu_custom_call" | custom-call | flops 4831838208 | bytes 6291456 | tf_op jit(solution)/shard_map/pallas_call | solution.py:262
  158.7 0.0 copy-start
  158.7 0.0 copy-start.3
  158.7 0.0 copy-start.4
  158.7 3.0 %convolution_convert_fusion = bf16[192,2048]{1,0:T(8,128)(2,1)} fusion(bf16[384,2048]{1,0:T(8,128)(2,1)} %bitcast.7, s32[192]{0:T(256)} %bitcast.10), kind=kOutput, calls=%fused_computation.2 | convolution fusion | flops 302456832 | bytes 2360064 | tf_op jit(solution)/shard_map/dot_general | solution.py:293
  161.7 0.0 copy-start.2
  161.7 0.0 copy-done
  161.7 0.0 copy-done.3
  161.7 0.0 copy-done.4
  161.7 1.5 fusion
  163.3 0.0 copy-done.2
  163.3 0.0 copy-start.1
  163.3 1.0 copy.13
  164.2 0.6 copy-done.1
  164.9 1.0 copy.14
Async XLA Ops:
  158.7 3.1 %copy-start = (bf16[16,24,2048]{2,1,0:T(8,128)(2,1)S(1)}, bf16[16,24,2048]{2,1,0:T(8,128)(2,1)}, u32[]{:S(2)}) copy-start(bf16[16,24,2048]{2,1,0:T(8,128)(2,1)} %get-tuple-element.10) | copy-start | bytes 4718596
  158.7 3.1 %copy-start.3 = (f32[192,1]{0,1:T(1,128)S(1)}, f32[192,1]{0,1:T(1,128)}, u32[]{:S(2)}) copy-start(f32[192,1]{0,1:T(1,128)} %param.8) | copy-start | bytes 2308
  158.7 3.1 %copy-start.4 = (s32[1,192]{1,0:T(1,128)S(1)}, s32[1,192]{1,0:T(1,128)}, u32[]{:S(2)}) copy-start(s32[1,192]{1,0:T(1,128)} %get-tuple-element.9) | copy-start | bytes 2308
  161.7 1.5 copy-start.2
  163.3 1.6 copy-start.1

commit v3 on v2

--- a/solution.py
+++ b/solution.py
@@ -30,8 +30,8 @@
 
 def expert_kernel(
     n_dp, n, cap, ids_ref, gate_ref, tokens_hbm, cotangent_hbm, up_ref, down_ref,
-    ret_out, ret_grad, gup_ref, gdown_ref, index_ref,
-    tokens_ref, cotangent_ref, tok_ref, cot_ref, arr_tok, arr_cot, x_all, c_all, up_all, down_all, preact_all, hid_all, pg_all,
+    rows_ref, tgrad_ref, gup_ref, gdown_ref,
+    ret_out, ret_grad, placer_t, tokens_ref, cotangent_ref, tok_ref, cot_ref, arr_tok, arr_cot, x_all, c_all, up_all, down_all, preact_all, hid_all, pg_all,
     placer_ref, left_t, out_buf, grad_buf, terms, landed, send_sem, recv_sem, dsend_sem, drecv_sem, local_sem,
 ):
     me = lax.axis_index("expert")
@@ -116,7 +116,6 @@
     )
     rank = jnp.sum(jnp.where(onehot, ranks, 0.0), axis=0, keepdims=True)
     index = ids * cap + rank.astype(jnp.int32)
-    index_ref[...] = index
     placer_ref[...] = (
         (lax.broadcasted_iota(jnp.int32, (n * cap, count), 0) == index)
         .astype(jnp.float32)
@@ -124,6 +123,9 @@
     )
     block = width // PLACE_BLOCKS
 
+    def gate_column():
+        return jnp.broadcast_to(gate_ref[...], (8, count)).T[:, :1]
+
     def place_tok(b):
         columns = pl.ds(pl.multiple_of(b * block, block), block)
         placed = dot_nn(placer_ref[...], tokens_ref[:, columns])
@@ -131,7 +133,7 @@
 
     def place_cot(b):
         columns = pl.ds(pl.multiple_of(b * block, block), block)
-        scaled = gate_ref[...] * cotangent_ref[:, columns].astype(jnp.float32)
+        scaled = gate_column() * cotangent_ref[:, columns].astype(jnp.float32)
         placed = dot_nn(placer_ref[...], scaled.astype(jnp.bfloat16))
         cot_ref[:, :, columns] = placed.reshape(n, cap, block).astype(jnp.bfloat16)
 
@@ -146,6 +148,20 @@
     load_cot.wait()
     each(0, PLACE_BLOCKS, place_cot)
     own_cot.start()
+    placer_t[...] = placer_ref[...].astype(jnp.float32).T.astype(jnp.bfloat16)
+
+    def pick(b, returned):
+        columns = pl.ds(pl.multiple_of(b * block, block), block)
+        values = returned[:, :, columns].astype(jnp.float32).reshape(n * cap, block)
+        return columns, dot_nn(placer_t[...], values.astype(jnp.bfloat16))
+
+    def pick_rows(b):
+        columns, picked = pick(b, ret_out)
+        rows_ref[:, columns] = (gate_column() * picked).astype(jnp.bfloat16)
+
+    def pick_grad(b):
+        columns, picked = pick(b, ret_grad)
+        tgrad_ref[:, columns] = picked.astype(jnp.bfloat16)
 
     own_tok.wait()
     for copy in own:
@@ -222,13 +238,14 @@
 
     weight_terms(TERM_DOWN, hid_all, c_all)
     weight_terms(TERM_UP, pg_all, x_all)
-    total(TERM_DOWN, gdown_ref)
-    total(TERM_UP, gup_ref)
-
     own_out.wait()
     own_grad.wait()
     each(1, n, lambda i: give_back(OUT, out_buf, ret_out, i).wait_recv())
+    each(0, PLACE_BLOCKS, pick_rows)
+    total(TERM_DOWN, gdown_ref)
+    total(TERM_UP, gup_ref)
     each(1, n, lambda i: give_back(GRAD, grad_buf, ret_grad, i).wait_recv())
+    each(0, PLACE_BLOCKS, pick_grad)
 
     def sent(i):
         dispatch(TOK, tok_ref, arr_tok, i).wait_send()
@@ -252,7 +269,7 @@
     count, width = tok.shape
     share = up.shape[1]
     ff, slot_total = share * n_dp, n * cap
-    slab = jax.ShapeDtypeStruct((n, cap, width), jnp.bfloat16)
+    result = jax.ShapeDtypeStruct((count, width), jnp.bfloat16)
     weight = jax.ShapeDtypeStruct((1, share, width), jnp.bfloat16)
     hbm, vmem = pl.BlockSpec(memory_space=pl.ANY), pl.BlockSpec(memory_space=pltpu.VMEM)
 
@@ -261,10 +278,11 @@
 
     return pl.pallas_call(
         functools.partial(expert_kernel, n_dp, n, cap),
-        out_shape=(slab, slab, weight, weight, jax.ShapeDtypeStruct((1, count), jnp.int32)),
+        out_shape=(result, result, weight, weight),
         in_specs=[vmem] * 2 + [hbm] * 4,
-        out_specs=(hbm, hbm, vmem, vmem, vmem),
+        out_specs=(vmem, vmem, vmem, vmem),
         scratch_shapes=[
+            half(n, cap, width), half(n, cap, width), half(count, slot_total),
             half(count, width), half(count, width),
             half(n, cap, width), half(n, cap, width),
             half(n, cap, width), half(n, cap, width),
@@ -289,26 +307,16 @@
     )(ids, gate, tok, cot, up, down)
 
 
-def contract_rows(left, right):
-    return lax.dot_general(
-        left, right, (((0,), (0,)), ((), ())), preferred_element_type=jnp.float32
-    )
-
-
 def per_device(tokens, routing, gate_scale, cotangent, up_weight, down_weight):
-    tok_count, width = tokens.shape
+    tok_count = tokens.shape[0]
     n_expert = lax.axis_size("expert")
     capacity = 2 * tok_count // n_expert
     capacity = -(-capacity // 8) * 8
-    slot_total = n_expert * capacity
-    returned, grad_back, grad_up, grad_down, slot_index = expert_call(
-        capacity, routing.reshape(1, tok_count), gate_scale, tokens, cotangent, up_weight, down_weight
-    )
-    placer = (jnp.arange(slot_total, dtype=jnp.int32)[:, None] == slot_index).astype(jnp.bfloat16)
-    picked = contract_rows(placer, returned.reshape(slot_total, width))
-    output_rows = (gate_scale * picked).astype(jnp.bfloat16)
-    token_grad = contract_rows(placer, grad_back.reshape(slot_total, width)).astype(jnp.bfloat16)
-    return (output_rows, token_grad, grad_up, grad_down)
+    row = (1, tok_count)
+    return expert_call(
+        capacity, routing.reshape(row), gate_scale.reshape(row), tokens, cotangent,
+        up_weight, down_weight,
+    )
 
 
 def solution(mesh):

time: 166 us -> 165 us (level)
  matrix products: 4.54 us -> 0 us
  local copies, waits for them, and re-layouts: 4.03 us -> 6.24 us
    dot_general x2 -> x0, matrix products: 4.54 us -> none  [contract_rows(): lax.dot_general(left, right, (((0,), (0,)), ((), ())), preferred_element_...]
    unnamed x13 -> x10, local copies, waits for them, and re-layouts: 4.03 us -> 6.24 us
where the time goes in v3:
time: 165 us
  Pallas kernels  158 us (96%)
  local copies, waits for them, and re-layouts  6.24 us (4%)
    pallas_call x1, Pallas kernels, expert_call(): pl.pallas_call(functools.partial(expert_kernel, n_dp, n, cap), out_shape=...  158 us
    unnamed x10, local copies, waits for them, and re-layouts  6.24 us

profile of v3, /device:TPU:11, one launch (start us, length us, event | category | flops | bytes accessed | tf_op | source)
XLA Modules:
  0.0 165.0 jit_solution(13657043702970006655)
XLA Ops:
  0.6 158.1 %shard_map.93 = (bf16[192,2048]{1,0:T(8,128)(2,1)}, bf16[192,2048]{1,0:T(8,128)(2,1)}, bf16[1,256,2048]{2,1,0:T(8,128)(2,1)}, bf16[1,256,2048]{2,1,0:T(8,128)(2,1)}) custom-call(s32[1,192]{1,0:T(1,128)} %bitcast.2, f32[1,192]{1,0:T(1,128)} %bitcast.3, bf16[192,2048]{1,0:T(8,128)(2,1)} %tokens_hbm.1, bf16[192,2048]{1,0:T(8,128)(2,1)} %cotangent_hbm.1, ...), custom_call_target="tpu_custom_call" | custom-call | flops 4831838208 | bytes 6291456 | tf_op jit(solution)/shard_map/pallas_call | solution.py:279
  158.7 0.0 copy-start.2
  158.7 2.2 %copy.14 = bf16[192,2048]{1,0:T(8,128)(2,1)} copy(bf16[192,2048]{1,0:T(8,128)(2,1)} %get-tuple-element.8) | data formatting | bytes 1572864
  160.9 0.0 copy-done.2
  160.9 0.0 copy-start.1
  160.9 0.9 copy.15
  161.8 0.6 copy-done.1
  162.4 0.0 copy-start
  162.4 1.0 copy.16
  163.4 0.6 copy-done
  164.0 1.0 copy.17
Async XLA Ops:
  158.7 2.2 %copy-start.2 = (bf16[192,2048]{1,0:T(8,128)(2,1)S(1)}, bf16[192,2048]{1,0:T(8,128)(2,1)}, u32[]{:S(2)}) copy-start(bf16[192,2048]{1,0:T(8,128)(2,1)} %get-tuple-element.9) | copy-start | bytes 2359300
  160.9 1.5 copy-start.1
  162.4 1.6 copy-start

commit v4 on v3

--- a/solution.py
+++ b/solution.py
@@ -298,7 +298,7 @@
             pltpu.SemaphoreType.DMA((6,)),
         ],
         compiler_params=pltpu.CompilerParams(
-            collective_id=0, has_side_effects=True, vmem_limit_bytes=60 * 1024 * 1024
+            collective_id=0, has_side_effects=True, vmem_limit_bytes=48 * 1024 * 1024
         ),
         cost_estimate=pl.CostEstimate(
             flops=12 * slot_total * width * ff, bytes_accessed=8 * slot_total * width,

time: 165 us -> 164 us (level)
  Pallas kernels: 158 us -> 156 us
    pallas_call x1, Pallas kernels: 158 us -> 156 us  [expert_call(): pl.pallas_call(functools.partial(expert_kernel, n_dp, n, cap), out_shape=...]
    unnamed x10 -> x12, local copies, waits for them, and re-layouts: 6.24 us -> 6.64 us
where the time goes in v4:
time: 164 us
  Pallas kernels  156 us (95%)
  local copies, waits for them, and re-layouts  6.64 us (4%)
    pallas_call x1, Pallas kernels, expert_call(): pl.pallas_call(functools.partial(expert_kernel, n_dp, n, cap), out_shape=...  156 us
    unnamed x12, local copies, waits for them, and re-layouts  6.64 us

profile of v4, /device:TPU:11, one launch (start us, length us, event | category | flops | bytes accessed | tf_op | source)
XLA Modules:
  0.0 163.5 jit_solution(11355214159721232085)
XLA Ops:
  0.6 0.0 copy-start.3
  0.6 0.0 copy-start.2
  0.7 0.7 copy-done.3
  1.3 0.0 copy-done.2
  1.3 0.0 copy-start
  1.3 1.1 copy-done
  2.5 0.0 copy-start.1
  2.5 1.1 copy-done.1
  3.6 156.2 %shard_map.93 = (bf16[192,2048]{1,0:T(8,128)(2,1)S(1)}, bf16[192,2048]{1,0:T(8,128)(2,1)S(1)}, bf16[1,256,2048]{2,1,0:T(8,128)(2,1)S(1)}, bf16[1,256,2048]{2,1,0:T(8,128)(2,1)S(1)}) custom-call(s32[1,192]{1,0:T(1,128)S(1)} %bitcast.2, f32[1,192]{1,0:T(1,128)S(1)} %bitcast.3, bf16[192,2048]{1,0:T(8,128)(2,1)S(1)} %copy-done, bf16[192,2048]{1,0:T(8,128)(2,1)S(1)} %copy-done.1, ...), custom_call_target="tpu_custom_call" | custom-call | flops 4831838208 | bytes 6291456 | tf_op jit(solution)/shard_map/pallas_call | solution.py:279
  159.8 0.9 copy.14
  160.7 0.9 copy.15
  161.6 1.0 copy.16
  162.5 1.0 copy.17
Async XLA Ops:
  0.6 0.7 copy-start.3
  0.6 0.7 copy-start.2
  1.3 1.1 copy-start
  2.5 1.1 copy-start.1
